TPU v7x, 256 devices: a whole 4x4x8 slice. The times are simulated.
256 devices in a mesh: section: 8 (over y, x_lo), dp: 16 (over z, core), rep: 2 (over x_hi).
Axes of the slice: x: 4 (x_hi: 2, x_lo: 2; x = x_hi * 2 + x_lo), y: 4, z: 8, core: 2. Of those that a mesh axis runs over, the one named last changes fastest.
Arguments:
- enc_weight: bfloat16 [8, 1280, 1280], P('section'), may hold values from -0.15625 to 0.15625
- dec_weight: bfloat16 [8, 1280, 1280], P('section'), may hold values from -0.25 to 0.25
- modulation: bfloat16 [8, 2, 256, 1280], P('section'), may hold values from -0.1796875 to 0.1796875
- enc_inputs: bfloat16 [8, 2, 32, 96, 1280], P('section', None, ('dp', 'rep')), may hold values from -6 to 6
- dec_inputs: bfloat16 [8, 2, 32, 96, 1280], P('section', None, ('dp', 'rep')), may hold values from -6 to 6
- cotangent: bfloat16 [2, 32, 96, 1280], P(None, ('dp', 'rep')), may hold values from -6 to 6
- timesteps: int32 [2, 32, 4], P(None, ('dp', 'rep')), may hold values from 0 to 999
Outputs:
- input_grads: bfloat16 [8, 2, 32, 96, 1280], P('section', None, ('dp', 'rep'))
- grams: float32 [8, 2, 1280, 1280], P('section', None, ('dp', 'rep'))
All inputs are finite; a program needn't handle non-finite values.
Results may differ from a plain program's by a relative error of at most 0.023.
Values may be sent and summed in bfloat16 or wider, within the bound.
A program may use at most 64 MiB of HBM per device.

v0:
```python
import jax
import jax.numpy as jnp
from jax import lax
from jax.sharding import PartitionSpec as P


def shifted(x, axis, by):
    devices = lax.axis_size(axis)
    pairs = [(i, i + by) for i in range(devices) if 0 <= i + by < devices]
    return lax.ppermute(x, axis, pairs)


def frame_gain(steps_frames, table):
    half = table.shape[0] // 2
    freqs = jnp.exp(-jnp.log(10000.0) * jnp.arange(half).astype(jnp.float32) / half)
    angles = steps_frames.astype(jnp.float32)[..., None] * freqs
    embedded = jnp.concatenate([jnp.sin(angles), jnp.cos(angles)], axis=-1)
    return 1.0 + jnp.einsum(
        "...e,ed->...d", embedded, table.astype(jnp.float32), precision=lax.Precision.HIGHEST
    )


def level_back(weight, inputs, row_gain, incoming):
    pre = jnp.dot(inputs, weight, preferred_element_type=jnp.float32) * row_gain
    sigma = jax.nn.sigmoid(pre)
    slope = sigma * (1.0 + pre * (1.0 - sigma))
    pre_grad = (incoming.astype(jnp.float32) * slope * row_gain).astype(jnp.bfloat16)
    back_grad = jnp.dot(pre_grad, weight.T, preferred_element_type=jnp.float32).astype(jnp.bfloat16)
    return (back_grad, pre_grad)


def send_up(message):
    return shifted(message, "section", 1)


def send_down(message):
    return shifted(message, "section", -1)


def body(enc_weight, dec_weight, modulation, enc_inputs, dec_inputs, cotangent, timesteps):
    section_idx = lax.axis_index("section")
    section_count = lax.axis_size("section")
    batches = cotangent.shape[0]
    tok_rows = cotangent.shape[2]
    channels = enc_weight.shape[2]
    frames = timesteps.shape[2]
    spatial = tok_rows // frames
    w_enc = enc_weight[0]
    w_dec = dec_weight[0]
    enc_rows = enc_inputs[0, :, 0]
    dec_rows = dec_inputs[0, :, 0]
    seeds = cotangent[:, 0]
    enc_gain = [
        jnp.repeat(frame_gain(timesteps[batch_idx, 0], modulation[0, 0]), spatial, axis=0)
        for batch_idx in range(batches)
    ]
    dec_gain = [
        jnp.repeat(frame_gain(timesteps[batch_idx, 0], modulation[0, 1]), spatial, axis=0)
        for batch_idx in range(batches)
    ]
    blank = jnp.zeros((tok_rows, channels), jnp.bfloat16)
    blanks = tuple((blank for batch_idx in range(batches)))

    def weight_grad(rows, grads):
        flat_rows = rows.reshape(batches * tok_rows, channels)
        flat_grads = jnp.stack(grads).reshape(batches * tok_rows, channels)
        return lax.dot_general(
            flat_rows, flat_grads, (((0,), (0,)), ((), ())), preferred_element_type=jnp.float32
        ).astype(jnp.bfloat16)

    dec_backs, dec_grads = (blanks, blanks)
    outputs, enc_grads = (blanks, blanks)
    for batch_idx in range(batches):
        decoder_plan = [(batch_idx, 0)]

        def decoder_advance(tick_idx, loop_state):
            received, backs_now, grads_now = loop_state
            backs_now = list(backs_now)
            grads_now = list(grads_now)
            outgoing = blank
            for batch_idx, offset in decoder_plan:
                active = section_idx == tick_idx - offset
                incoming = jnp.where(section_idx == 0, seeds[batch_idx], received)
                back_grad, pre_grad = lax.cond(
                    active,
                    lambda: level_back(w_dec, dec_rows[batch_idx], dec_gain[batch_idx], incoming),
                    lambda: (backs_now[batch_idx], grads_now[batch_idx]),
                )
                outgoing = jnp.where(active, back_grad, outgoing)
                backs_now[batch_idx] = back_grad
                grads_now[batch_idx] = pre_grad
            return (send_up(outgoing), tuple(backs_now), tuple(grads_now))

        decoder_final = lax.fori_loop(
            0, section_count, decoder_advance, (blank, dec_backs, dec_grads)
        )
        dec_backs = decoder_final[1]
        dec_grads = decoder_final[2]
        plan = [(batch_idx, 0)]
        skips = dec_backs

        def encoder_advance(tick_idx, loop_state):
            received, outs_now, grads_now = loop_state
            outs_now = list(outs_now)
            grads_now = list(grads_now)
            outgoing = blank
            from_above = jnp.where(section_idx == section_count - 1, blank, received)
            for batch_idx, offset in plan:
                active = section_idx == section_count - 1 - (tick_idx - offset)
                combined = (
                    skips[batch_idx].astype(jnp.float32) + from_above.astype(jnp.float32)
                ).astype(jnp.bfloat16)
                back_grad, pre_grad = lax.cond(
                    active,
                    lambda: level_back(w_enc, enc_rows[batch_idx], enc_gain[batch_idx], combined),
                    lambda: (outs_now[batch_idx], grads_now[batch_idx]),
                )
                outgoing = jnp.where(active, back_grad, outgoing)
                outs_now[batch_idx] = back_grad
                grads_now[batch_idx] = pre_grad
            return (send_down(outgoing), tuple(outs_now), tuple(grads_now))

        final = lax.fori_loop(0, section_count, encoder_advance, (blank, outputs, enc_grads))
        outputs = final[1]
        enc_grads = final[2]
    dp_count = lax.axis_size("dp")
    rep_count = lax.axis_size("rep")
    denom = channels * batches * tok_rows * dp_count * rep_count
    stacked = jnp.stack(
        [weight_grad(enc_rows, enc_grads), weight_grad(dec_rows, dec_grads)]
    ).astype(jnp.float32)
    summed = lax.psum_scatter(
        stacked.astype(jnp.bfloat16), ("dp", "rep"), scatter_dimension=2, tiled=True
    )
    grams = (
        jnp.einsum(
            "scr,scn->srn",
            summed,
            lax.all_gather(summed, ("dp", "rep"), axis=2, tiled=True),
            preferred_element_type=jnp.float32,
        )
        / denom
    )[None]
    input_grads = jnp.stack(outputs)[None, :, None]
    return (input_grads, grams)


def solution(mesh):
    return jax.shard_map(
        body,
        mesh=mesh,
        in_specs=(
            P("section", None, None),
            P("section", None, None),
            P("section", None, None, None),
            P("section", None, ("dp", "rep"), None, None),
            P("section", None, ("dp", "rep"), None, None),
            P(None, ("dp", "rep"), None, None),
            P(None, ("dp", "rep"), None),
        ),
        out_specs=(
            P("section", None, ("dp", "rep"), None, None),
            P("section", None, ("dp", "rep"), None),
        ),
        check_vma=False,
    )
```

profile of v0, /device:TPU:1, one launch (start us, length us, event | category | flops | bytes accessed | tf_op | source)
XLA Modules:
  0.0 751.9 jit_solution(9348222948741186782)
XLA Ops:
  17.3 88.4 %while.78 = (s32[]{:T(128)}, bf16[96,1280]{1,0:T(8,128)(2,1)}, bf16[96,1280]{1,0:T(8,128)(2,1)S(1)}, bf16[96,1280]{1,0:T(8,128)(2,1)}, s32[]{:T(128)}, /*index=5...) while((s32[]{:T(128)}, bf16[96,1280]{1,0:T(8,128)(2,1)}, ...), condition=%wide.region_11.12_spmd.clone, body=%wide.region_8.11_spmd.clone.sunk | while | flops 630988800 | bytes 11490072 | solution.py:94
  18.9 3.2 conditional.14
  29.7 8.1 %collective-permute-start.2 = (bf16[96,1280]{1,0:T(8,128)(2,1)}, bf16[96,1280]{1,0:T(8,128)(2,1)}, u32[]{:S(2)}, u32[]{:S(2)}) collective-permute-start(bf16[96,1280]{1,0:T(8,128)(2,1)} %broadcast_select_fusion.10), channel_id=1, source_target_pairs={{0,32},{32,64},{64,96},{96,128},{128,160},{160,192},{192,224},{1,3... | collective-permute-start | bytes 737288 | tf_op jit(solution)/shard_map/while/body/eval_jaxpr/ppermute | solution.py:10
  42.8 4.5 collective-permute-start.2
  52.3 6.7 collective-permute-start.2
  64.0 5.4 collective-permute-start.2
  74.4 5.4 collective-permute-start.2
  84.8 5.4 collective-permute-start.2
  90.2 3.2 collective-permute-done.2
  95.7 5.7 collective-permute-start.2
  101.4 4.3 collective-permute-done.2
  107.9 99.2 %while.76 = (s32[]{:T(128)}, bf16[96,1280]{1,0:T(8,128)(2,1)}, bf16[96,1280]{1,0:T(8,128)(2,1)}, bf16[96,1280]{1,0:T(8,128)(2,1)}, s32[]{:T(128)}, /*index=5*/pr...) while((s32[]{:T(128)}, bf16[96,1280]{1,0:T(8,128)(2,1)}, ...), condition=%wide.region_3.4_spmd.clone, body=%wide.region_0.3_spmd.clone.sunk | while | flops 630988800 | bytes 11490072 | solution.py:94
  109.5 3.9 conditional.12
  122.0 10.1 %collective-permute-start = (bf16[96,1280]{1,0:T(8,128)(2,1)}, bf16[96,1280]{1,0:T(8,128)(2,1)}, u32[]{:S(2)}, u32[]{:S(2)}) collective-permute-start(bf16[96,1280]{1,0:T(8,128)(2,1)} %broadcast_select_fusion.8), channel_id=1, source_target_pairs={{0,32},{32,64},{64,96},{96,128},{128,160},{160,192},{192,224},{1,3... | collective-permute-start | bytes 737288 | tf_op jit(solution)/shard_map/while/body/eval_jaxpr/ppermute | solution.py:10
  137.0 4.7 collective-permute-start
  146.7 10.3 %collective-permute-start = (bf16[96,1280]{1,0:T(8,128)(2,1)}, bf16[96,1280]{1,0:T(8,128)(2,1)}, u32[]{:S(2)}, u32[]{:S(2)}) collective-permute-start(bf16[96,1280]{1,0:T(8,128)(2,1)} %broadcast_select_fusion.8), channel_id=1, source_target_pairs={{0,32},{32,64},{64,96},{96,128},{128,160},{160,192},{192,224},{1,3... | collective-permute-start | bytes 737288 | tf_op jit(solution)/shard_map/while/body/eval_jaxpr/ppermute | solution.py:10
  157.0 4.8 collective-permute-done
  164.1 4.8 collective-permute-start
  173.9 7.8 %collective-permute-start = (bf16[96,1280]{1,0:T(8,128)(2,1)}, bf16[96,1280]{1,0:T(8,128)(2,1)}, u32[]{:S(2)}, u32[]{:S(2)}) collective-permute-start(bf16[96,1280]{1,0:T(8,128)(2,1)} %broadcast_select_fusion.8), channel_id=1, source_target_pairs={{0,32},{32,64},{64,96},{96,128},{128,160},{160,192},{192,224},{1,3... | collective-permute-start | bytes 737288 | tf_op jit(solution)/shard_map/while/body/eval_jaxpr/ppermute | solution.py:10
  186.6 5.7 collective-permute-start
  197.3 7.1 collective-permute-start
  209.0 120.2 %while.79 = (s32[]{:T(128)}, bf16[96,1280]{1,0:T(8,128)(2,1)S(1)}, bf16[96,1280]{1,0:T(8,128)(2,1)S(1)}, bf16[96,1280]{1,0:T(8,128)(2,1)}, s32[]{:T(128)}, /*ind...) while((s32[]{:T(128)}, bf16[96,1280]{1,0:T(8,128)(2,1)S(1)}, ...), condition=%wide.region_15.16_spmd.clone, body=%wide.region_12.15_spmd.clone.sunk | while | flops 631480320 | bytes 24105244 | solution.py:123
  211.3 9.5 %collective-permute-done.3 = bf16[96,1280]{1,0:T(8,128)(2,1)S(1)} collective-permute-done((bf16[96,1280]{1,0:T(8,128)(2,1)S(1)}, bf16[96,1280]{1,0:T(8,128)(2,1)S(1)}, u32[]{:S(2)}, u32[]{:S(2)}) %collective-permute-start.3) | collective-permute-done | bytes 245792 | tf_op jit(solution)/shard_map/while/body/eval_jaxpr/ppermute | solution.py:10
  222.9 7.4 collective-permute-done.3
  232.5 7.0 collective-permute-done.3
  241.7 11.3 %collective-permute-done.3 = bf16[96,1280]{1,0:T(8,128)(2,1)S(1)} collective-permute-done((bf16[96,1280]{1,0:T(8,128)(2,1)S(1)}, bf16[96,1280]{1,0:T(8,128)(2,1)S(1)}, u32[]{:S(2)}, u32[]{:S(2)}) %collective-permute-start.3) | collective-permute-done | bytes 245792 | tf_op jit(solution)/shard_map/while/body/eval_jaxpr/ppermute | solution.py:10
  255.2 6.7 collective-permute-done.3
  264.1 6.1 collective-permute-done.3
  272.4 43.3 %collective-permute-done.3 = bf16[96,1280]{1,0:T(8,128)(2,1)S(1)} collective-permute-done((bf16[96,1280]{1,0:T(8,128)(2,1)S(1)}, bf16[96,1280]{1,0:T(8,128)(2,1)S(1)}, u32[]{:S(2)}, u32[]{:S(2)}) %collective-permute-start.3) | collective-permute-done | bytes 245792 | tf_op jit(solution)/shard_map/while/body/eval_jaxpr/ppermute | solution.py:10
  316.5 5.8 conditional.15
  316.5 3.7 multiply_convert_fusion.3
  323.6 5.6 collective-permute-done.3
  330.0 90.8 %while.77 = (s32[]{:T(128)}, bf16[96,1280]{1,0:T(8,128)(2,1)S(1)}, bf16[96,1280]{1,0:T(8,128)(2,1)S(1)}, bf16[96,1280]{1,0:T(8,128)(2,1)}, s32[]{:T(128)}, /*ind...) while((s32[]{:T(128)}, bf16[96,1280]{1,0:T(8,128)(2,1)S(1)}, ...), condition=%wide.region_7.8_spmd.clone, body=%wide.region_4.7_spmd.clone.sunk | while | flops 631480320 | bytes 24105244 | solution.py:123
  331.5 5.6 collective-permute-done.1
  338.6 8.5 %collective-permute-done.1 = bf16[96,1280]{1,0:T(8,128)(2,1)S(1)} collective-permute-done((bf16[96,1280]{1,0:T(8,128)(2,1)S(1)}, bf16[96,1280]{1,0:T(8,128)(2,1)S(1)}, u32[]{:S(2)}, u32[]{:S(2)}) %collective-permute-start.1) | collective-permute-done | bytes 245792 | tf_op jit(solution)/shard_map/while/body/eval_jaxpr/ppermute | solution.py:10
  348.7 5.6 collective-permute-done.1
  355.8 8.3 %collective-permute-done.1 = bf16[96,1280]{1,0:T(8,128)(2,1)S(1)} collective-permute-done((bf16[96,1280]{1,0:T(8,128)(2,1)S(1)}, bf16[96,1280]{1,0:T(8,128)(2,1)S(1)}, u32[]{:S(2)}, u32[]{:S(2)}) %collective-permute-start.1) | collective-permute-done | bytes 245792 | tf_op jit(solution)/shard_map/while/body/eval_jaxpr/ppermute | solution.py:10
  365.6 6.6 collective-permute-done.1
  373.7 5.6 collective-permute-done.1
  380.8 25.6 %collective-permute-done.1 = bf16[96,1280]{1,0:T(8,128)(2,1)S(1)} collective-permute-done((bf16[96,1280]{1,0:T(8,128)(2,1)S(1)}, bf16[96,1280]{1,0:T(8,128)(2,1)S(1)}, u32[]{:S(2)}, u32[]{:S(2)}) %collective-permute-start.1) | collective-permute-done | bytes 245792 | tf_op jit(solution)/shard_map/while/body/eval_jaxpr/ppermute | solution.py:10
  406.5 5.8 conditional.13
  406.6 3.7 multiply_convert_fusion.1
  413.6 7.2 collective-permute-done.1
  425.8 46.9 %copy.9 = bf16[2,1280,1280]{1,0,2:T(2,128)(2,1)S(1)} copy(bf16[2,1280,1280]{1,2,0:T(8,128)(2,1)S(1)} %pad_maximum_fusion) | data formatting | bytes 13107200
  472.7 4.0 copy.11
  476.8 161.4 %reduce-scatter.4.cloned.1.call-done = bf16[40,2560]{1,0:T(8,128)(2,1)} async-done(((bf16[1280,2560]{1,0:T(8,128)(2,1)}), bf16[40,2560]{1,0:T(8,128)(2,1)}) %reduce-scatter.4.cloned.1.call-update) | async-done | bytes 204816
  640.7 98.7 %all-gather.2.cloned.1.call-done = bf16[2,1280,1280]{1,2,0:T(8,128)(2,1)} async-done(((bf16[2,1280,40]{1,2,0:T(8,128)(2,1)}), bf16[2,1280,1280]{1,2,0:T(8,128)(2,1)}) %all-gather.2.cloned.1.call-update) | async-done | bytes 6553616 | tf_op jit(solution)/shard_map/all_gather | solution.py:139
  739.4 5.6 fusion.18
  (190 shorter events, 139.0 us)
Async XLA Ops:
  7.2 10.2 %copy-start = (bf16[1,1280,1280]{2,1,0:T(8,128)(2,1)S(1)}, bf16[1,1280,1280]{2,1,0:T(8,128)(2,1)}, u32[]{:S(2)}) copy-start(bf16[1,1280,1280]{2,1,0:T(8,128)(2,1)} %param.24) | copy-start | bytes 9830404
  7.2 631.0 %reduce-scatter.4.cloned.1.call-start = ((), (), s32[]{:S(2)}) async-start(), calls=%async_computation.2 | async-start | bytes 6758400
  20.9 1.2 copy-start.4
  22.8 4.7 collective-permute-start.2
  29.7 10.8 %collective-permute-start.2 = (bf16[96,1280]{1,0:T(8,128)(2,1)}, bf16[96,1280]{1,0:T(8,128)(2,1)}, u32[]{:S(2)}, u32[]{:S(2)}) collective-permute-start(bf16[96,1280]{1,0:T(8,128)(2,1)} %broadcast_select_fusion.10), channel_id=1, source_target_pairs={{0,32},{32,64},{64,96},{96,128},{128,160},{160,192},{192,224},{1,3... | collective-permute-start | bytes 737288 | tf_op jit(solution)/shard_map/while/body/eval_jaxpr/ppermute | solution.py:10
  42.8 7.2 collective-permute-start.2
  52.3 9.5 %collective-permute-start.2 = (bf16[96,1280]{1,0:T(8,128)(2,1)}, bf16[96,1280]{1,0:T(8,128)(2,1)}, u32[]{:S(2)}, u32[]{:S(2)}) collective-permute-start(bf16[96,1280]{1,0:T(8,128)(2,1)} %broadcast_select_fusion.10), channel_id=1, source_target_pairs={{0,32},{32,64},{64,96},{96,128},{128,160},{160,192},{192,224},{1,3... | collective-permute-start | bytes 737288 | tf_op jit(solution)/shard_map/while/body/eval_jaxpr/ppermute | solution.py:10
  64.0 8.1 %collective-permute-start.2 = (bf16[96,1280]{1,0:T(8,128)(2,1)}, bf16[96,1280]{1,0:T(8,128)(2,1)}, u32[]{:S(2)}, u32[]{:S(2)}) collective-permute-start(bf16[96,1280]{1,0:T(8,128)(2,1)} %broadcast_select_fusion.10), channel_id=1, source_target_pairs={{0,32},{32,64},{64,96},{96,128},{128,160},{160,192},{192,224},{1,3... | collective-permute-start | bytes 737288 | tf_op jit(solution)/shard_map/while/body/eval_jaxpr/ppermute | solution.py:10
  74.4 8.1 %collective-permute-start.2 = (bf16[96,1280]{1,0:T(8,128)(2,1)}, bf16[96,1280]{1,0:T(8,128)(2,1)}, u32[]{:S(2)}, u32[]{:S(2)}) collective-permute-start(bf16[96,1280]{1,0:T(8,128)(2,1)} %broadcast_select_fusion.10), channel_id=1, source_target_pairs={{0,32},{32,64},{64,96},{96,128},{128,160},{160,192},{192,224},{1,3... | collective-permute-start | bytes 737288 | tf_op jit(solution)/shard_map/while/body/eval_jaxpr/ppermute | solution.py:10
  84.8 8.6 %collective-permute-start.2 = (bf16[96,1280]{1,0:T(8,128)(2,1)}, bf16[96,1280]{1,0:T(8,128)(2,1)}, u32[]{:S(2)}, u32[]{:S(2)}) collective-permute-start(bf16[96,1280]{1,0:T(8,128)(2,1)} %broadcast_select_fusion.10), channel_id=1, source_target_pairs={{0,32},{32,64},{64,96},{96,128},{128,160},{160,192},{192,224},{1,3... | collective-permute-start | bytes 737288 | tf_op jit(solution)/shard_map/while/body/eval_jaxpr/ppermute | solution.py:10
  95.7 10.0 %collective-permute-start.2 = (bf16[96,1280]{1,0:T(8,128)(2,1)}, bf16[96,1280]{1,0:T(8,128)(2,1)}, u32[]{:S(2)}, u32[]{:S(2)}) collective-permute-start(bf16[96,1280]{1,0:T(8,128)(2,1)} %broadcast_select_fusion.10), channel_id=1, source_target_pairs={{0,32},{32,64},{64,96},{96,128},{128,160},{160,192},{192,224},{1,3... | collective-permute-start | bytes 737288 | tf_op jit(solution)/shard_map/while/body/eval_jaxpr/ppermute | solution.py:10
  111.5 1.9 copy-start.5
  115.0 4.7 collective-permute-start
  122.0 12.8 %collective-permute-start = (bf16[96,1280]{1,0:T(8,128)(2,1)}, bf16[96,1280]{1,0:T(8,128)(2,1)}, u32[]{:S(2)}, u32[]{:S(2)}) collective-permute-start(bf16[96,1280]{1,0:T(8,128)(2,1)} %broadcast_select_fusion.8), channel_id=1, source_target_pairs={{0,32},{32,64},{64,96},{96,128},{128,160},{160,192},{192,224},{1,3... | collective-permute-start | bytes 737288 | tf_op jit(solution)/shard_map/while/body/eval_jaxpr/ppermute | solution.py:10
  137.0 7.4 collective-permute-start
  146.7 15.1 %collective-permute-start = (bf16[96,1280]{1,0:T(8,128)(2,1)}, bf16[96,1280]{1,0:T(8,128)(2,1)}, u32[]{:S(2)}, u32[]{:S(2)}) collective-permute-start(bf16[96,1280]{1,0:T(8,128)(2,1)} %broadcast_select_fusion.8), channel_id=1, source_target_pairs={{0,32},{32,64},{64,96},{96,128},{128,160},{160,192},{192,224},{1,3... | collective-permute-start | bytes 737288 | tf_op jit(solution)/shard_map/while/body/eval_jaxpr/ppermute | solution.py:10
  164.1 7.5 %collective-permute-start = (bf16[96,1280]{1,0:T(8,128)(2,1)}, bf16[96,1280]{1,0:T(8,128)(2,1)}, u32[]{:S(2)}, u32[]{:S(2)}) collective-permute-start(bf16[96,1280]{1,0:T(8,128)(2,1)} %broadcast_select_fusion.8), channel_id=1, source_target_pairs={{0,32},{32,64},{64,96},{96,128},{128,160},{160,192},{192,224},{1,3... | collective-permute-start | bytes 737288 | tf_op jit(solution)/shard_map/while/body/eval_jaxpr/ppermute | solution.py:10
  173.9 10.5 %collective-permute-start = (bf16[96,1280]{1,0:T(8,128)(2,1)}, bf16[96,1280]{1,0:T(8,128)(2,1)}, u32[]{:S(2)}, u32[]{:S(2)}) collective-permute-start(bf16[96,1280]{1,0:T(8,128)(2,1)} %broadcast_select_fusion.8), channel_id=1, source_target_pairs={{0,32},{32,64},{64,96},{96,128},{128,160},{160,192},{192,224},{1,3... | collective-permute-start | bytes 737288 | tf_op jit(solution)/shard_map/while/body/eval_jaxpr/ppermute | solution.py:10
  186.6 8.4 %collective-permute-start = (bf16[96,1280]{1,0:T(8,128)(2,1)}, bf16[96,1280]{1,0:T(8,128)(2,1)}, u32[]{:S(2)}, u32[]{:S(2)}) collective-permute-start(bf16[96,1280]{1,0:T(8,128)(2,1)} %broadcast_select_fusion.8), channel_id=1, source_target_pairs={{0,32},{32,64},{64,96},{96,128},{128,160},{160,192},{192,224},{1,3... | collective-permute-start | bytes 737288 | tf_op jit(solution)/shard_map/while/body/eval_jaxpr/ppermute | solution.py:10
  197.3 9.9 %collective-permute-start = (bf16[96,1280]{1,0:T(8,128)(2,1)}, bf16[96,1280]{1,0:T(8,128)(2,1)}, u32[]{:S(2)}, u32[]{:S(2)}) collective-permute-start(bf16[96,1280]{1,0:T(8,128)(2,1)} %broadcast_select_fusion.8), channel_id=1, source_target_pairs={{0,32},{32,64},{64,96},{96,128},{128,160},{160,192},{192,224},{1,3... | collective-permute-start | bytes 737288 | tf_op jit(solution)/shard_map/while/body/eval_jaxpr/ppermute | solution.py:10
  209.0 121.0 %copy-start.3 = (bf16[96,1280]{1,0:T(8,128)(2,1)S(1)}, bf16[96,1280]{1,0:T(8,128)(2,1)}, u32[]{:S(2)}) copy-start(bf16[96,1280]{1,0:T(8,128)(2,1)} %get-tuple-element.1481) | copy-start | bytes 737284
  210.0 10.8 %collective-permute-start.3 = (bf16[96,1280]{1,0:T(8,128)(2,1)S(1)}, bf16[96,1280]{1,0:T(8,128)(2,1)S(1)}, u32[]{:S(2)}, u32[]{:S(2)}) collective-permute-start(bf16[96,1280]{1,0:T(8,128)(2,1)S(1)} %broadcast_select_fusion.11), channel_id=1, source_target_pairs={{32,0},{64,32},{96,64},{128,96},{160,128},{192,160},{224,192},{33,... | collective-permute-start | bytes 737288 | tf_op jit(solution)/shard_map/while/body/eval_jaxpr/ppermute | solution.py:10
  221.6 8.7 %collective-permute-start.3 = (bf16[96,1280]{1,0:T(8,128)(2,1)S(1)}, bf16[96,1280]{1,0:T(8,128)(2,1)S(1)}, u32[]{:S(2)}, u32[]{:S(2)}) collective-permute-start(bf16[96,1280]{1,0:T(8,128)(2,1)S(1)} %broadcast_select_fusion.11), channel_id=1, source_target_pairs={{32,0},{64,32},{96,64},{128,96},{160,128},{192,160},{224,192},{33,... | collective-permute-start | bytes 737288 | tf_op jit(solution)/shard_map/while/body/eval_jaxpr/ppermute | solution.py:10
  231.2 8.3 %collective-permute-start.3 = (bf16[96,1280]{1,0:T(8,128)(2,1)S(1)}, bf16[96,1280]{1,0:T(8,128)(2,1)S(1)}, u32[]{:S(2)}, u32[]{:S(2)}) collective-permute-start(bf16[96,1280]{1,0:T(8,128)(2,1)S(1)} %broadcast_select_fusion.11), channel_id=1, source_target_pairs={{32,0},{64,32},{96,64},{128,96},{160,128},{192,160},{224,192},{33,... | collective-permute-start | bytes 737288 | tf_op jit(solution)/shard_map/while/body/eval_jaxpr/ppermute | solution.py:10
  240.4 12.6 %collective-permute-start.3 = (bf16[96,1280]{1,0:T(8,128)(2,1)S(1)}, bf16[96,1280]{1,0:T(8,128)(2,1)S(1)}, u32[]{:S(2)}, u32[]{:S(2)}) collective-permute-start(bf16[96,1280]{1,0:T(8,128)(2,1)S(1)} %broadcast_select_fusion.11), channel_id=1, source_target_pairs={{32,0},{64,32},{96,64},{128,96},{160,128},{192,160},{224,192},{33,... | collective-permute-start | bytes 737288 | tf_op jit(solution)/shard_map/while/body/eval_jaxpr/ppermute | solution.py:10
  253.9 8.0 %collective-permute-start.3 = (bf16[96,1280]{1,0:T(8,128)(2,1)S(1)}, bf16[96,1280]{1,0:T(8,128)(2,1)S(1)}, u32[]{:S(2)}, u32[]{:S(2)}) collective-permute-start(bf16[96,1280]{1,0:T(8,128)(2,1)S(1)} %broadcast_select_fusion.11), channel_id=1, source_target_pairs={{32,0},{64,32},{96,64},{128,96},{160,128},{192,160},{224,192},{33,... | collective-permute-start | bytes 737288 | tf_op jit(solution)/shard_map/while/body/eval_jaxpr/ppermute | solution.py:10
  262.8 7.4 collective-permute-start.3
  271.1 44.6 %collective-permute-start.3 = (bf16[96,1280]{1,0:T(8,128)(2,1)S(1)}, bf16[96,1280]{1,0:T(8,128)(2,1)S(1)}, u32[]{:S(2)}, u32[]{:S(2)}) collective-permute-start(bf16[96,1280]{1,0:T(8,128)(2,1)S(1)} %broadcast_select_fusion.11), channel_id=1, source_target_pairs={{32,0},{64,32},{96,64},{128,96},{160,128},{192,160},{224,192},{33,... | collective-permute-start | bytes 737288 | tf_op jit(solution)/shard_map/while/body/eval_jaxpr/ppermute | solution.py:10
  316.5 3.7 copy-start.1
  322.3 6.9 collective-permute-start.3
  330.2 6.9 collective-permute-start.1
  337.3 9.8 %collective-permute-start.1 = (bf16[96,1280]{1,0:T(8,128)(2,1)S(1)}, bf16[96,1280]{1,0:T(8,128)(2,1)S(1)}, u32[]{:S(2)}, u32[]{:S(2)}) collective-permute-start(bf16[96,1280]{1,0:T(8,128)(2,1)S(1)} %broadcast_select_fusion.9), channel_id=1, source_target_pairs={{32,0},{64,32},{96,64},{128,96},{160,128},{192,160},{224,192},{33,... | collective-permute-start | bytes 737288 | tf_op jit(solution)/shard_map/while/body/eval_jaxpr/ppermute | solution.py:10
  347.4 6.9 collective-permute-start.1
  354.5 9.6 %collective-permute-start.1 = (bf16[96,1280]{1,0:T(8,128)(2,1)S(1)}, bf16[96,1280]{1,0:T(8,128)(2,1)S(1)}, u32[]{:S(2)}, u32[]{:S(2)}) collective-permute-start(bf16[96,1280]{1,0:T(8,128)(2,1)S(1)} %broadcast_select_fusion.9), channel_id=1, source_target_pairs={{32,0},{64,32},{96,64},{128,96},{160,128},{192,160},{224,192},{33,... | collective-permute-start | bytes 737288 | tf_op jit(solution)/shard_map/while/body/eval_jaxpr/ppermute | solution.py:10
  364.3 7.9 %collective-permute-start.1 = (bf16[96,1280]{1,0:T(8,128)(2,1)S(1)}, bf16[96,1280]{1,0:T(8,128)(2,1)S(1)}, u32[]{:S(2)}, u32[]{:S(2)}) collective-permute-start(bf16[96,1280]{1,0:T(8,128)(2,1)S(1)} %broadcast_select_fusion.9), channel_id=1, source_target_pairs={{32,0},{64,32},{96,64},{128,96},{160,128},{192,160},{224,192},{33,... | collective-permute-start | bytes 737288 | tf_op jit(solution)/shard_map/while/body/eval_jaxpr/ppermute | solution.py:10
  372.4 6.9 collective-permute-start.1
  379.5 26.9 %collective-permute-start.1 = (bf16[96,1280]{1,0:T(8,128)(2,1)S(1)}, bf16[96,1280]{1,0:T(8,128)(2,1)S(1)}, u32[]{:S(2)}, u32[]{:S(2)}) collective-permute-start(bf16[96,1280]{1,0:T(8,128)(2,1)S(1)} %broadcast_select_fusion.9), channel_id=1, source_target_pairs={{32,0},{64,32},{96,64},{128,96},{160,128},{192,160},{224,192},{33,... | collective-permute-start | bytes 737288 | tf_op jit(solution)/shard_map/while/body/eval_jaxpr/ppermute | solution.py:10
  406.5 3.7 copy-start.2
  412.3 8.5 %collective-permute-start.1 = (bf16[96,1280]{1,0:T(8,128)(2,1)S(1)}, bf16[96,1280]{1,0:T(8,128)(2,1)S(1)}, u32[]{:S(2)}, u32[]{:S(2)}) collective-permute-start(bf16[96,1280]{1,0:T(8,128)(2,1)S(1)} %broadcast_select_fusion.9), channel_id=1, source_target_pairs={{32,0},{64,32},{96,64},{128,96},{160,128},{192,160},{224,192},{33,... | collective-permute-start | bytes 737288 | tf_op jit(solution)/shard_map/while/body/eval_jaxpr/ppermute | solution.py:10
  420.8 3.3 copy-start.6
  476.7 262.7 %all-gather.2.cloned.1.call-start = ((), (), s32[]{:S(2)}) async-start(), calls=%async_computation.1 | async-start | bytes 6758400 | tf_op jit(solution)/shard_map/all_gather | solution.py:139
Sparse Core Ops, SparseCore 0:
  476.8 161.3 reduce-scatter.3
  641.9 97.4 all-gather.1
where the time goes:
time: 755 us; the launch traced here: 752 us
  waiting for transfers between devices  478 us (63%)
  starting transfers between devices  116 us (15%)
  local copies, waits for them, and re-layouts  88.7 us (12%)
  matrix products  34.9 us (5%)
  other arithmetic  18.6 us (2%)
  between operations  14.2 us (2%)
    ppermute x32, waiting for transfers between devices, shifted(): return lax.ppermute(x, axis, pairs)  218 us
    unnamed x3, waiting for transfers between devices  161 us
    ppermute x32, starting transfers between devices, shifted(): return lax.ppermute(x, axis, pairs)  116 us
    all_gather x1, waiting for transfers between devices, body(): lax.all_gather(summed, ('dp', 'rep'), axis=2, tiled=True)  98.7 us
    unnamed x10, local copies, waits for them, and re-layouts  52.6 us
    broadcast_in_dim x16, local copies, waits for them, and re-layouts, body(): jnp.repeat(frame_gain(timesteps[batch_idx, 0], modulation[0, 1]), spatial...  24.6 us
  transfers between devices with their start and end apart: 34, of which 34 were waited for; matrix products, arithmetic and copies ran while one was open for 0% of the time, Pallas kernels for 0%

commit v1 on v0

v1 whole, which is shorter than its diff:
```python
import jax
import jax.numpy as jnp
from jax import lax
from jax.experimental import pallas as pl
from jax.experimental.pallas import tpu as pltpu
from jax.sharding import PartitionSpec as P

MESH = pl.DeviceIdType.MESH
F32 = jnp.float32
BF16 = jnp.bfloat16

C = 1280
HALF = C // 2
ROWS = 192
PIECE = 32
PIECES = ROWS // PIECE
FRAME = 24
LEVELS = 8
BLOCK = 80
OUT_ROWS = 40
PHASES = 6
DENOM = 7864320.0
ENC, DEC = 0, 1


def kernel(
    emb_ref, enc_w, dec_w, mod_hbm, enc_u, dec_u, cot_hbm, out_ref, gram_ref,
    w, wt, mod, u, sg, chain_in, back, delta, gains,
    u4, d4, part, from_rep, from_z, g, gram_acc, own_gram, send_gram, recv_gram,
    load_sem, chain_s, chain_r, u_s, u_r, d_s, d_r, x_s, x_r, z_s, z_r,
    az_s, az_r, ax_s, ax_r, ac_s, ac_r, f_s, f_r,
):
    s = lax.axis_index("section")
    dp = lax.axis_index("dp")
    r = lax.axis_index("rep")
    z, c = dp // 2, dp % 2
    zp, zg = z % 2, z // 2
    up = {"section": lax.rem(s + 1, LEVELS)}
    down = {"section": lax.rem(s + LEVELS - 1, LEVELS)}
    z_other = z + 1 - 2 * zp
    sibling = {"dp": z * 2 + 1 - c}
    pair_same = {"dp": z_other * 2 + c}
    pair_cross = {"dp": z_other * 2 + 1 - c}
    rep_other = {"rep": 1 - r}
    quad = [sibling, pair_same, pair_cross]
    quad_core = [1 - c, c, 1 - c]
    quad_zp = [zp, 1 - zp, 1 - zp]
    zg_of = [lax.rem(zg + 1 + j, 4) for j in range(3)]
    z_group = [{"dp": (zg_of[j] * 2 + zp) * 2 + c} for j in range(3)]
    slot = zp * 2 + c
    quad_slot = [zp * 2 + 1 - c, (1 - zp) * 2 + c, (1 - zp) * 2 + 1 - c]

    def remote(src, dst, ss, rs, dev):
        return pltpu.make_async_remote_copy(
            src_ref=src, dst_ref=dst, send_sem=ss, recv_sem=rs, device_id=dev, device_id_type=MESH
        )

    def load(src, dst, a, b):
        return pltpu.make_async_copy(src, dst, load_sem.at[a, b])

    load(dec_u, u.at[DEC], DEC, 1).start()
    load(enc_u, u.at[ENC], ENC, 1).start()
    load(dec_w, w.at[DEC], DEC, 0).start()
    load(mod_hbm.at[DEC], mod.at[DEC], DEC, 2).start()
    cot_load = pltpu.make_async_copy(cot_hbm, chain_in.at[DEC], load_sem.at[0, 3])

    @pl.when(s == 0)
    def _():
        cot_load.start()

    load(enc_w, w.at[ENC], ENC, 0).start()
    load(mod_hbm.at[ENC], mod.at[ENC], ENC, 2).start()

    barrier = pltpu.get_barrier_semaphore()
    partners = [up, down, rep_other] + quad + z_group
    for dev in partners:
        pl.semaphore_signal(barrier, inc=1, device_id=dev, device_id_type=MESH)

    @pl.when(s == LEVELS - 1)
    def _():
        chain_in[ENC] = jnp.zeros((ROWS, C), BF16)

    def col(h):
        return pl.ds(pl.multiple_of(h * HALF, HALF), HALF)

    def rows(start, size, unit):
        return pl.ds(pl.multiple_of(start, unit), size)

    def prep(side):
        load(dec_w, w.at[side], side, 0).wait()
        load(mod_hbm.at[DEC], mod.at[side], side, 2).wait()
        sg[side] = jnp.dot(u[side], w[side], preferred_element_type=F32)
        e = emb_ref[...]
        hi = e.astype(BF16)
        rest = e - hi.astype(F32)
        mid = rest.astype(BF16)
        low = (rest - mid.astype(F32)).astype(BF16)
        table = mod[side]
        gains[...] = 1.0 + (
            jnp.dot(hi, table, preferred_element_type=F32)
            + (jnp.dot(mid, table, preferred_element_type=F32) + jnp.dot(low, table, preferred_element_type=F32))
        )

        def frame(f, carry):
            at = rows(f * FRAME, FRAME, 8)
            gain = gains[pl.ds(f, 1), :]
            pre = sg[side, at, :] * gain
            sigma = jax.nn.sigmoid(pre)
            sg[side, at, :] = sigma * (1.0 + pre * (1.0 - sigma)) * gain
            return carry

        lax.fori_loop(0, ROWS // FRAME, frame, 0)
        wt[side] = w[side].T

    def chain_copy(side, m):
        at = rows(m * PIECE, PIECE, PIECE)
        dev = {"section": jnp.where(side == DEC, lax.rem(s + 1, LEVELS), lax.rem(s + LEVELS - 1, LEVELS))}
        return remote(back.at[side, at], chain_in.at[side, at], chain_s.at[side, m], chain_r.at[side, m], dev)

    def delta_copy(side, m, q):
        at = rows(m * PIECE, PIECE, PIECE)
        there = rows(slot * ROWS + m * PIECE, PIECE, PIECE)
        return remote(
            delta.at[side, at, col(quad_core[q])], d4.at[side, there], d_s.at[side, q, m], d_r.at[side, q, m], quad[q]
        )

    def u_copy(side, q):
        there = rows(slot * ROWS, ROWS, ROWS)
        return remote(u.at[side, :, col(quad_zp[q])], u4.at[side, there], u_s.at[side, q], u_r.at[side, q], quad[q])

    def level(side, m, incoming):
        at = rows(m * PIECE, PIECE, PIECE)
        d = (incoming * sg[side, at, :]).astype(BF16)
        delta[side, at, :] = d
        back[side, at, :] = jnp.dot(d, wt[side], preferred_element_type=F32).astype(BF16)

    def share_delta(side, m):
        for q in range(3):
            delta_copy(side, m, q).start()
        at = rows(m * PIECE, PIECE, PIECE)
        d4[side, rows(slot * ROWS + m * PIECE, PIECE, PIECE), :] = delta[side, at, col(c)]

    def piece_rows(rr, zz):
        return rows((rr * 4 + zz) * BLOCK, BLOCK, 16)

    def x_copy(side, zz):
        return remote(
            part.at[side, piece_rows(1 - r, zz)], from_rep.at[side, rows(zz * BLOCK, BLOCK, 16)],
            x_s.at[side, zz], x_r.at[side, zz], rep_other,
        )

    def z_copy(side, j):
        return remote(
            part.at[side, piece_rows(r, zg_of[j])], from_z.at[side, 2 - j], z_s.at[side, j], z_r.at[side, 2 - j], z_group[j]
        )

    def g_piece(side, rr, zz, cc):
        return g.at[side, piece_rows(rr, zz), col(cc)]

    def az_copy(side, j):
        p = g_piece(side, r, zg, c)
        return remote(p, p, az_s.at[side, j], az_r.at[side, 2 - j], z_group[j])

    def ax_copy(side, zz):
        p = g_piece(side, r, zz, c)
        return remote(p, p, ax_s.at[side, zz], ax_r.at[side, zz], rep_other)

    def ac_copy(side, rr, zz):
        p = g_piece(side, rr, zz, c)
        return remote(p, p, ac_s.at[side, rr * 4 + zz], ac_r.at[side, rr * 4 + zz], sibling)

    def f_copy(side):
        return remote(send_gram.at[side], recv_gram.at[side], f_s.at[side], f_r.at[side], pair_same)

    def window(side, base):
        start = jnp.minimum((base // 128) * 128, C - 256)
        cols = pl.ds(pl.multiple_of(start, 128), 256)
        gram_acc[...] = lax.dot_general(
            g[side, :, cols], g[side], (((0,), (0,)), ((), ())), preferred_element_type=F32
        )
        return gram_acc[rows(base - start, OUT_ROWS, 8), :]

    def phase(p, side):
        @pl.when(p == -1)
        def _():
            prep(side)

        @pl.when(p == 0)
        def _():
            for q in range(3):
                u_copy(side, q).wait_recv()

                def one(m, carry):
                    delta_copy(side, m, q).wait_recv()
                    return carry

                lax.fori_loop(0, PIECES, one, 0)
            part[side] = lax.dot_general(
                u4[side], d4[side], (((0,), (0,)), ((), ())), preferred_element_type=F32
            ).astype(BF16)
            for j in range(3):
                x_copy(side, zg_of[j]).start()
            x_copy(side, zg).start()

        @pl.when(p == 1)
        def _():
            for j in range(3):
                x_copy(side, zg_of[j]).wait_recv()
                at = piece_rows(r, zg_of[j])
                part[side, at, :] = (
                    part[side, at, :].astype(F32)
                    + from_rep[side, rows(zg_of[j] * BLOCK, BLOCK, 16), :].astype(F32)
                ).astype(BF16)
                z_copy(side, j).start()

        @pl.when(p == 2)
        def _():
            x_copy(side, zg).wait_recv()
            total = part[side, piece_rows(r, zg), :].astype(F32) + from_rep[
                side, rows(zg * BLOCK, BLOCK, 16), :
            ].astype(F32)
            for j in range(3):
                z_copy(side, 2 - j).wait_recv()
                total = total + from_z[side, j].astype(F32)
            g[side, piece_rows(r, zg), col(c)] = total.astype(BF16)
            for j in range(3):
                az_copy(side, j).start()
            ax_copy(side, zg).start()
            ac_copy(side, r, zg).start()

        @pl.when(p == 3)
        def _():
            for j in range(3):
                zz = lax.rem(zg + 1 + j, 4)
                az_copy(side, 2 - j).wait_recv()
                ax_copy(side, zz).start()
                ac_copy(side, r, zz).start()

        @pl.when(p == 4)
        def _():
            ax_copy(side, zg).wait_recv()
            ac_copy(side, 1 - r, zg).start()
            for j in range(3):
                ax_copy(side, zg_of[j]).wait_recv()
                ac_copy(side, 1 - r, zg_of[j]).start()
            for rr in range(2):
                for zz in range(4):
                    ac_copy(side, rr, zz).wait_recv()
            send_gram[side] = window(side, 160 * z_other + 80 * c + 40 * r)
            f_copy(side).start()
            own_gram[side] = window(side, 160 * z + 80 * c + 40 * r)

        @pl.when(p == 5)
        def _():
            f_copy(side).wait_recv()
            gram_ref[side] = (own_gram[side] + recv_gram[side]) / DENOM

    early = jnp.where(
        s <= 2, PHASES, jnp.where(s == 3, 3, jnp.where(s == 4, 2, jnp.where(s == 5, 1, 0)))
    )

    def step(i, carry):
        last = s == LEVELS - 1
        is_chain = (i >= 0) & (i < 2 * PIECES)
        is_dec = is_chain & jnp.where(last, i % 2 == 0, i < PIECES)
        is_enc = is_chain & jnp.where(last, i % 2 == 1, i >= PIECES)
        m = jnp.where(last, i // 2, i % PIECES)

        @pl.when(is_dec)
        def _():
            @pl.when(s > 0)
            def _():
                chain_copy(DEC, m).wait_recv()

            @pl.when((s == 0) & (m == 0))
            def _():
                cot_load.wait()

            at = rows(m * PIECE, PIECE, PIECE)
            level(DEC, m, chain_in[DEC, at, :].astype(F32))

            @pl.when(s < LEVELS - 1)
            def _():
                chain_copy(DEC, m).start()

            share_delta(DEC, m)

        @pl.when(is_enc)
        def _():
            @pl.when(s < LEVELS - 1)
            def _():
                chain_copy(ENC, m).wait_recv()

            at = rows(m * PIECE, PIECE, PIECE)
            both = (back[DEC, at, :].astype(F32) + chain_in[ENC, at, :].astype(F32)).astype(BF16)
            level(ENC, m, both.astype(F32))

            @pl.when(s > 0)
            def _():
                chain_copy(ENC, m).start()

            share_delta(ENC, m)
            out_ref[at, :] = back[ENC, at, :]

        middle = i == PIECES - 1
        late = i >= 2 * PIECES
        n = jnp.where(middle, jnp.where(s == 0, early + 1, early), jnp.where(late, 2, 0))

        def event(j, carry):
            p = jnp.where(middle, jnp.where(s == 0, j - 1, j), i - 2 * PIECES)
            side = jnp.where(middle, jnp.where(p < 0, ENC, DEC), 1 - j)
            done = late & (side == DEC) & (p < early)

            @pl.when(jnp.logical_not(done))
            def _():
                phase(p, side)

            return carry

        lax.fori_loop(0, n, event, 0)

        return carry

    load(dec_u, u.at[DEC], DEC, 1).wait()
    load(enc_u, u.at[ENC], ENC, 1).wait()

    def prepare(j, carry):
        prep(1 - j)
        return carry

    lax.fori_loop(0, jnp.where(s == 0, 1, 2), prepare, 0)
    pl.semaphore_wait(barrier, len(partners))
    for side in (DEC, ENC):
        for q in range(3):
            u_copy(side, q).start()
        u4[side, rows(slot * ROWS, ROWS, ROWS), :] = u[side, :, col(zp)]
    lax.fori_loop(0, 2 * PIECES + PHASES, step, 0)

    for side in (DEC, ENC):
        for q in range(3):
            u_copy(side, q).wait_send()

            def sent(m, carry):
                delta_copy(side, m, q).wait_send()
                return carry

            lax.fori_loop(0, PIECES, sent, 0)

        def chained(m, carry):
            chain_copy(side, m).wait_send()
            return carry

        @pl.when((s < LEVELS - 1) if side == DEC else (s > 0))
        def _():
            lax.fori_loop(0, PIECES, chained, 0)

        for j in range(3):
            z_copy(side, j).wait_send()
            az_copy(side, j).wait_send()
        for zz in range(4):
            x_copy(side, zz).wait_send()
            ax_copy(side, zz).wait_send()
            for rr in range(2):
                ac_copy(side, rr, zz).wait_send()
        f_copy(side).wait_send()


def body(enc_weight, dec_weight, modulation, enc_inputs, dec_inputs, cotangent, timesteps):
    half = modulation.shape[2] // 2
    freqs = jnp.exp(-jnp.log(10000.0) * jnp.arange(half).astype(F32) / half)
    angles = timesteps.reshape(-1).astype(F32)[:, None] * freqs
    emb = jnp.concatenate([jnp.sin(angles), jnp.cos(angles)], axis=-1)
    dma = pltpu.SemaphoreType.DMA
    out, grams = pl.pallas_call(
        kernel,
        name="unet_backward",
        out_shape=(jax.ShapeDtypeStruct((ROWS, C), BF16), jax.ShapeDtypeStruct((2, OUT_ROWS, C), F32)),
        in_specs=[pl.BlockSpec(memory_space=pltpu.VMEM)] + [pl.BlockSpec(memory_space=pl.ANY)] * 6,
        out_specs=(pl.BlockSpec(memory_space=pltpu.VMEM), pl.BlockSpec(memory_space=pltpu.VMEM)),
        scratch_shapes=[
            pltpu.VMEM((2, C, C), BF16), pltpu.VMEM((2, C, C), BF16), pltpu.VMEM((2, 256, C), BF16),
            pltpu.VMEM((2, ROWS, C), BF16), pltpu.VMEM((2, ROWS, C), F32), pltpu.VMEM((2, ROWS, C), BF16),
            pltpu.VMEM((2, ROWS, C), BF16), pltpu.VMEM((2, ROWS, C), BF16), pltpu.VMEM((8, C), F32),
            pltpu.VMEM((2, 4 * ROWS, HALF), BF16), pltpu.VMEM((2, 4 * ROWS, HALF), BF16),
            pltpu.VMEM((2, HALF, HALF), BF16), pltpu.VMEM((2, HALF // 2, HALF), BF16),
            pltpu.VMEM((2, 3, BLOCK, HALF), BF16), pltpu.VMEM((2, HALF, C), BF16), pltpu.VMEM((256, C), F32),
            pltpu.VMEM((2, OUT_ROWS, C), F32), pltpu.VMEM((2, OUT_ROWS, C), F32), pltpu.VMEM((2, OUT_ROWS, C), F32),
            dma((2, 4)), dma((2, PIECES)), dma((2, PIECES)), dma((2, 3)), dma((2, 3)),
            dma((2, 3, PIECES)), dma((2, 3, PIECES)), dma((2, 4)), dma((2, 4)), dma((2, 3)), dma((2, 3)),
            dma((2, 3)), dma((2, 3)), dma((2, 4)), dma((2, 4)), dma((2, 8)), dma((2, 8)), dma((2,)), dma((2,)),
        ],
        compiler_params=pltpu.CompilerParams(
            collective_id=0, has_side_effects=True, vmem_limit_bytes=60 * 1024 * 1024
        ),
    )(
        emb, enc_weight.reshape(C, C), dec_weight.reshape(C, C), modulation.reshape(2, 256, C),
        enc_inputs.reshape(ROWS, C), dec_inputs.reshape(ROWS, C), cotangent.reshape(ROWS, C),
    )
    return out.reshape(1, 2, 1, ROWS // 2, C), grams[None]


def solution(mesh):
    return jax.shard_map(
        body,
        mesh=mesh,
        in_specs=(
            P("section", None, None),
            P("section", None, None),
            P("section", None, None, None),
            P("section", None, ("dp", "rep"), None, None),
            P("section", None, ("dp", "rep"), None, None),
            P(None, ("dp", "rep"), None, None),
            P(None, ("dp", "rep"), None),
        ),
        out_specs=(
            P("section", None, ("dp", "rep"), None, None),
            P("section", None, ("dp", "rep"), None),
        ),
        check_vma=False,
    )
```

time: 755 us -> 166 us (0.22)
  waiting for transfers between devices: 478 us -> 0 us
  Pallas kernels: 0 us -> 160 us
  starting transfers between devices: 116 us -> 0 us
  local copies, waits for them, and re-layouts: 88.7 us -> 3.7 us
  matrix products: 34.9 us -> 0 us
  other arithmetic: 18.6 us -> 1.42 us
  between operations: 14.2 us -> 0.65 us
    ppermute x32 -> x0, waiting for transfers between devices: 218 us -> none  [shifted(): return lax.ppermute(x, axis, pairs)]
    unnamed x3 -> x0, waiting for transfers between devices: 161 us -> none
    pallas_call x0 -> x1, Pallas kernels: none -> 160 us  [body(): pl.pallas_call(kernel, name='unet_backward', out_shape=(jax.ShapeDtypeStr...]
    ppermute x32 -> x0, starting transfers between devices: 116 us -> none  [shifted(): return lax.ppermute(x, axis, pairs)]
    all_gather x1 -> x0, waiting for transfers between devices: 98.7 us -> none  [body(): lax.all_gather(summed, ('dp', 'rep'), axis=2, tiled=True)]
    unnamed x10 -> x2, local copies, waits for them, and re-layouts: 52.6 us -> 3.62 us
    broadcast_in_dim x44 -> x0, local copies, waits for them, and re-layouts: 36 us -> none  [the longest x16 24.6 us: body(): jnp.repeat(frame_gain(timesteps[batch_idx, 0], modulation[0, 1]), spatial...]
    dot_general x15 -> x0, matrix products: 34.9 us -> none  [the longest x4 11.3 us: level_back(): pre = jnp.dot(inputs, weight, preferred_element_type=jnp.float32) * row_gain]
  transfers between devices with their start and end apart: 34 -> 0, of which waited for: 34 -> 0; matrix products, arithmetic and copies ran while one was open for 0% -> 0% of each run, Pallas kernels for 0% -> 0%
where the time goes in v1:
time: 166 us
  Pallas kernels  160 us (96%)
  local copies, waits for them, and re-layouts  3.7 us (2%)
    pallas_call x1, Pallas kernels, body(): pl.pallas_call(kernel, name='unet_backward', out_shape=(jax.ShapeDtypeStr...  160 us
    unnamed x2, local copies, waits for them, and re-layouts  3.62 us

profile of v1, /device:TPU:1, one launch (start us, length us, event | category | flops | bytes accessed | tf_op | source)
XLA Modules:
  0.0 166.1 jit_solution(12910856478267814209)
XLA Ops:
  0.6 0.7 convert_reduce_fusion
  1.3 0.1 convert_element_type.18
  1.4 0.1 multiply_sine_fusion
  1.5 0.6 pad_maximum_fusion.emb_ref
  2.1 160.4 %unet_backward.1 = (bf16[192,1280]{1,0:T(8,128)(2,1)}, f32[2,40,1280]{2,1,0:T(8,128)}) custom-call(f32[8,256]{1,0:T(8,128)} %pad_maximum_fusion.emb_ref, bf16[1280,1280]{1,0:T(8,128)(2,1)} %bitcast.10, bf16[1280,1280]{1,0:T(8,128)(2,1)} %bitcast.11, bf16[2,256,1280]{2,1,0:T(8,128)(2,1)} %bitcast.12, bf16[192,1280]{1,0:T(8,128)(2,1)} %bitcast.14, ...), custom_call_target="tpu_custom_call" | custom-call | tf_op jit(solution)/shard_map/unet_backward/pallas_call | solution.py:374
  162.5 1.8 %copy.12 = bf16[1,2,1,96,1280]{4,3,2,1,0:T(8,128)(2,1)} copy(bf16[1,2,1,96,1280]{4,3,2,1,0:T(8,128)(2,1)} %bitcast.13) | data formatting | bytes 983040
  164.3 1.8 %copy.13 = f32[1,2,40,1280]{3,2,1,0:T(8,128)} copy(f32[1,2,40,1280]{3,2,1,0:T(8,128)} %bitcast.17) | data formatting | bytes 819200
  (1 shorter events, 0.0 us)

commit v2 on v1

--- a/solution.py
+++ b/solution.py
@@ -14,11 +14,14 @@
 ROWS = 192
 PIECE = 32
 PIECES = ROWS // PIECE
+SPLIT = 2
+PART = C // SPLIT
 FRAME = 24
 LEVELS = 8
 BLOCK = 80
 OUT_ROWS = 40
-PHASES = 6
+PHASES = 7
+EARLY = (6, 6, 5, 4, 2, 2, 1, 1)
 DENOM = 7864320.0
 ENC, DEC = 0, 1
 
@@ -26,9 +29,9 @@
 def kernel(
     emb_ref, enc_w, dec_w, mod_hbm, enc_u, dec_u, cot_hbm, out_ref, gram_ref,
     w, wt, mod, u, sg, chain_in, back, delta, gains,
-    u4, d4, part, from_rep, from_z, g, gram_acc, own_gram, send_gram, recv_gram,
+    u4, u4t, d4, part, from_rep, from_z, g, gram_acc, own_gram, send_gram, recv_gram,
     load_sem, chain_s, chain_r, u_s, u_r, d_s, d_r, x_s, x_r, z_s, z_r,
-    az_s, az_r, ax_s, ax_r, ac_s, ac_r, f_s, f_r,
+    az_s, az_r, ac_s, ac_r, f_s, f_r,
 ):
     s = lax.axis_index("section")
     dp = lax.axis_index("dp")
@@ -47,6 +50,7 @@
     quad_zp = [zp, 1 - zp, 1 - zp]
     zg_of = [lax.rem(zg + 1 + j, 4) for j in range(3)]
     z_group = [{"dp": (zg_of[j] * 2 + zp) * 2 + c} for j in range(3)]
+    gram_peer = [{"dp": z_other * 2 + c, "rep": 1 - r}, pair_same, rep_other]
     slot = zp * 2 + c
     quad_slot = [zp * 2 + 1 - c, (1 - zp) * 2 + c, (1 - zp) * 2 + 1 - c]
 
@@ -72,7 +76,7 @@
     load(mod_hbm.at[ENC], mod.at[ENC], ENC, 2).start()
 
     barrier = pltpu.get_barrier_semaphore()
-    partners = [up, down, rep_other] + quad + z_group
+    partners = [up, down, gram_peer[0], rep_other] + quad + z_group
     for dev in partners:
         pl.semaphore_signal(barrier, inc=1, device_id=dev, device_id_type=MESH)
 
@@ -112,10 +116,13 @@
         lax.fori_loop(0, ROWS // FRAME, frame, 0)
         wt[side] = w[side].T
 
-    def chain_copy(side, m):
+    def chain_copy(side, m, k):
         at = rows(m * PIECE, PIECE, PIECE)
+        cols = pl.ds(k * PART, PART)
         dev = {"section": jnp.where(side == DEC, lax.rem(s + 1, LEVELS), lax.rem(s + LEVELS - 1, LEVELS))}
-        return remote(back.at[side, at], chain_in.at[side, at], chain_s.at[side, m], chain_r.at[side, m], dev)
+        return remote(
+            back.at[side, at, cols], chain_in.at[side, at, cols], chain_s.at[side, m, k], chain_r.at[side, m, k], dev
+        )
 
     def delta_copy(side, m, q):
         at = rows(m * PIECE, PIECE, PIECE)
@@ -128,11 +135,17 @@
         there = rows(slot * ROWS, ROWS, ROWS)
         return remote(u.at[side, :, col(quad_zp[q])], u4.at[side, there], u_s.at[side, q], u_r.at[side, q], quad[q])
 
-    def level(side, m, incoming):
+    def level(side, m, incoming, sends):
         at = rows(m * PIECE, PIECE, PIECE)
         d = (incoming * sg[side, at, :]).astype(BF16)
         delta[side, at, :] = d
-        back[side, at, :] = jnp.dot(d, wt[side], preferred_element_type=F32).astype(BF16)
+        for k in range(SPLIT):
+            cols = pl.ds(k * PART, PART)
+            back[side, at, cols] = jnp.dot(d, wt[side, :, cols], preferred_element_type=F32).astype(BF16)
+
+            @pl.when(sends)
+            def _():
+                chain_copy(side, m, k).start()
 
     def share_delta(side, m):
         for q in range(3):
@@ -154,31 +167,28 @@
             part.at[side, piece_rows(r, zg_of[j])], from_z.at[side, 2 - j], z_s.at[side, j], z_r.at[side, 2 - j], z_group[j]
         )
 
-    def g_piece(side, rr, zz, cc):
-        return g.at[side, piece_rows(rr, zz), col(cc)]
+    def g_piece(side, zz):
+        return g.at[side, rows(zz * BLOCK, BLOCK, 16), col(c)]
 
     def az_copy(side, j):
-        p = g_piece(side, r, zg, c)
+        p = g_piece(side, zg)
         return remote(p, p, az_s.at[side, j], az_r.at[side, 2 - j], z_group[j])
 
-    def ax_copy(side, zz):
-        p = g_piece(side, r, zz, c)
-        return remote(p, p, ax_s.at[side, zz], ax_r.at[side, zz], rep_other)
-
-    def ac_copy(side, rr, zz):
-        p = g_piece(side, rr, zz, c)
-        return remote(p, p, ac_s.at[side, rr * 4 + zz], ac_r.at[side, rr * 4 + zz], sibling)
-
-    def f_copy(side):
-        return remote(send_gram.at[side], recv_gram.at[side], f_s.at[side], f_r.at[side], pair_same)
-
-    def window(side, base):
+    def ac_copy(side, zz):
+        p = g_piece(side, zz)
+        return remote(p, p, ac_s.at[side, zz], ac_r.at[side, zz], sibling)
+
+    def f_copy(side, j):
+        return remote(send_gram.at[side, j], recv_gram.at[side, j], f_s.at[side, j], f_r.at[side, j], gram_peer[j])
+
+    def multiply_gathered(side, zz):
+        base = 160 * zz + 80 * c
         start = jnp.minimum((base // 128) * 128, C - 256)
         cols = pl.ds(pl.multiple_of(start, 128), 256)
         gram_acc[...] = lax.dot_general(
             g[side, :, cols], g[side], (((0,), (0,)), ((), ())), preferred_element_type=F32
         )
-        return gram_acc[rows(base - start, OUT_ROWS, 8), :]
+        return base - start
 
     def phase(p, side):
         @pl.when(p == -1)
@@ -189,20 +199,28 @@
         def _():
             for q in range(3):
                 u_copy(side, q).wait_recv()
+            u4t[side] = u4[side].T
+
+        @pl.when(p == 1)
+        def _():
+            for q in range(3):
 
                 def one(m, carry):
                     delta_copy(side, m, q).wait_recv()
                     return carry
 
                 lax.fori_loop(0, PIECES, one, 0)
-            part[side] = lax.dot_general(
-                u4[side], d4[side], (((0,), (0,)), ((), ())), preferred_element_type=F32
-            ).astype(BF16)
-            for j in range(3):
-                x_copy(side, zg_of[j]).start()
-            x_copy(side, zg).start()
-
-        @pl.when(p == 1)
+            for rr in (1 - r, r):
+                at = rows(rr * (HALF // 2), HALF // 2, 16)
+                part[side, at, :] = jnp.dot(
+                    u4t[side, at, :], d4[side], preferred_element_type=F32
+                ).astype(BF16)
+                if rr is not r:
+                    for j in range(3):
+                        x_copy(side, zg_of[j]).start()
+                    x_copy(side, zg).start()
+
+        @pl.when(p == 2)
         def _():
             for j in range(3):
                 x_copy(side, zg_of[j]).wait_recv()
@@ -213,7 +231,7 @@
                 ).astype(BF16)
                 z_copy(side, j).start()
 
-        @pl.when(p == 2)
+        @pl.when(p == 3)
         def _():
             x_copy(side, zg).wait_recv()
             total = part[side, piece_rows(r, zg), :].astype(F32) + from_rep[
@@ -222,93 +240,104 @@
             for j in range(3):
                 z_copy(side, 2 - j).wait_recv()
                 total = total + from_z[side, j].astype(F32)
-            g[side, piece_rows(r, zg), col(c)] = total.astype(BF16)
+            g[side, rows(zg * BLOCK, BLOCK, 16), col(c)] = total.astype(BF16)
             for j in range(3):
                 az_copy(side, j).start()
-            ax_copy(side, zg).start()
-            ac_copy(side, r, zg).start()
-
-        @pl.when(p == 3)
+            ac_copy(side, zg).start()
+
+        @pl.when(p == 4)
         def _():
             for j in range(3):
-                zz = lax.rem(zg + 1 + j, 4)
                 az_copy(side, 2 - j).wait_recv()
-                ax_copy(side, zz).start()
-                ac_copy(side, r, zz).start()
-
-        @pl.when(p == 4)
-        def _():
-            ax_copy(side, zg).wait_recv()
-            ac_copy(side, 1 - r, zg).start()
+                ac_copy(side, zg_of[j]).start()
+
+        @pl.when(p == 5)
+        def _():
+            for zz in range(4):
+                ac_copy(side, zz).wait_recv()
+
+            def there(k, carry):
+                offset = multiply_gathered(side, jnp.where(k == 0, z_other, z))
+
+                @pl.when(k == 0)
+                def _():
+                    for j, rr in ((0, 1 - r), (1, r)):
+                        send_gram[side, j] = gram_acc[rows(offset + 40 * rr, OUT_ROWS, 8), :].astype(BF16)
+                        f_copy(side, j).start()
+
+                @pl.when(k == 1)
+                def _():
+                    send_gram[side, 2] = gram_acc[rows(offset + 40 * (1 - r), OUT_ROWS, 8), :].astype(BF16)
+                    f_copy(side, 2).start()
+                    own_gram[side] = gram_acc[rows(offset + 40 * r, OUT_ROWS, 8), :]
+
+                return carry
+
+            lax.fori_loop(0, 2, there, 0)
+
+        @pl.when(p == 6)
+        def _():
+            gram = own_gram[side]
             for j in range(3):
-                ax_copy(side, zg_of[j]).wait_recv()
-                ac_copy(side, 1 - r, zg_of[j]).start()
-            for rr in range(2):
-                for zz in range(4):
-                    ac_copy(side, rr, zz).wait_recv()
-            send_gram[side] = window(side, 160 * z_other + 80 * c + 40 * r)
-            f_copy(side).start()
-            own_gram[side] = window(side, 160 * z + 80 * c + 40 * r)
-
-        @pl.when(p == 5)
-        def _():
-            f_copy(side).wait_recv()
-            gram_ref[side] = (own_gram[side] + recv_gram[side]) / DENOM
-
-    early = jnp.where(
-        s <= 2, PHASES, jnp.where(s == 3, 3, jnp.where(s == 4, 2, jnp.where(s == 5, 1, 0)))
-    )
-
-    def step(i, carry):
+                f_copy(side, j).wait_recv()
+                gram = gram + recv_gram[side, j].astype(F32)
+            gram_ref[side] = gram / DENOM
+
+    early = jnp.int32(0)
+    for level_index, count in enumerate(EARLY):
+        early = jnp.where(s == level_index, count, early)
+
+    def step(t, carry):
+        i = jnp.maximum(t, 1) - 1
         last = s == LEVELS - 1
-        is_chain = (i >= 0) & (i < 2 * PIECES)
+        is_chain = (t > 0) & (t <= 2 * PIECES)
         is_dec = is_chain & jnp.where(last, i % 2 == 0, i < PIECES)
         is_enc = is_chain & jnp.where(last, i % 2 == 1, i >= PIECES)
-        m = jnp.where(last, i // 2, i % PIECES)
+        m = jnp.where(last, lax.div(i, 2), lax.rem(i, PIECES))
 
         @pl.when(is_dec)
         def _():
             @pl.when(s > 0)
             def _():
-                chain_copy(DEC, m).wait_recv()
+                for k in range(SPLIT):
+                    chain_copy(DEC, m, k).wait_recv()
 
             @pl.when((s == 0) & (m == 0))
             def _():
                 cot_load.wait()
 
             at = rows(m * PIECE, PIECE, PIECE)
-            level(DEC, m, chain_in[DEC, at, :].astype(F32))
-
+            level(DEC, m, chain_in[DEC, at, :].astype(F32), s < LEVELS - 1)
+            share_delta(DEC, m)
+
+        @pl.when(is_enc)
+        def _():
             @pl.when(s < LEVELS - 1)
             def _():
-                chain_copy(DEC, m).start()
-
-            share_delta(DEC, m)
-
-        @pl.when(is_enc)
-        def _():
-            @pl.when(s < LEVELS - 1)
-            def _():
-                chain_copy(ENC, m).wait_recv()
+                for k in range(SPLIT):
+                    chain_copy(ENC, m, k).wait_recv()
 
             at = rows(m * PIECE, PIECE, PIECE)
             both = (back[DEC, at, :].astype(F32) + chain_in[ENC, at, :].astype(F32)).astype(BF16)
-            level(ENC, m, both.astype(F32))
-
-            @pl.when(s > 0)
-            def _():
-                chain_copy(ENC, m).start()
-
+            level(ENC, m, both.astype(F32), s > 0)
             share_delta(ENC, m)
             out_ref[at, :] = back[ENC, at, :]
 
-        middle = i == PIECES - 1
-        late = i >= 2 * PIECES
-        n = jnp.where(middle, jnp.where(s == 0, early + 1, early), jnp.where(late, 2, 0))
+        first = t == 0
+        middle = t == PIECES
+        late = t > 2 * PIECES
+        front = s < 4
+        lead = jnp.where(s == 0, 2, 1)
+        n = jnp.where(
+            first,
+            jnp.where(front, 0, 2),
+            jnp.where(middle, jnp.where(front, lead + early, early - 1), jnp.where(late, 2, 0)),
+        )
 
         def event(j, carry):
-            p = jnp.where(middle, jnp.where(s == 0, j - 1, j), i - 2 * PIECES)
-            side = jnp.where(middle, jnp.where(p < 0, ENC, DEC), 1 - j)
+            p_middle = jnp.where(front, jnp.where(j < lead, j + 1 - lead, j - lead), j + 1)
+            p = jnp.where(first, 0, jnp.where(middle, p_middle, t - 2 * PIECES))
+            side = jnp.where(middle, jnp.where(front & (j < lead), ENC, DEC), 1 - j)
             done = late & (side == DEC) & (p < early)
 
             @pl.when(jnp.logical_not(done))
@@ -347,7 +376,8 @@
             lax.fori_loop(0, PIECES, sent, 0)
 
         def chained(m, carry):
-            chain_copy(side, m).wait_send()
+            for k in range(SPLIT):
+                chain_copy(side, m, k).wait_send()
             return carry
 
         @pl.when((s < LEVELS - 1) if side == DEC else (s > 0))
@@ -357,12 +387,10 @@
         for j in range(3):
             z_copy(side, j).wait_send()
             az_copy(side, j).wait_send()
+            f_copy(side, j).wait_send()
         for zz in range(4):
             x_copy(side, zz).wait_send()
-            ax_copy(side, zz).wait_send()
-            for rr in range(2):
-                ac_copy(side, rr, zz).wait_send()
-        f_copy(side).wait_send()
+            ac_copy(side, zz).wait_send()
 
 
 def body(enc_weight, dec_weight, modulation, enc_inputs, dec_inputs, cotangent, timesteps):
@@ -381,20 +409,22 @@
             pltpu.VMEM((2, C, C), BF16), pltpu.VMEM((2, C, C), BF16), pltpu.VMEM((2, 256, C), BF16),
             pltpu.VMEM((2, ROWS, C), BF16), pltpu.VMEM((2, ROWS, C), F32), pltpu.VMEM((2, ROWS, C), BF16),
             pltpu.VMEM((2, ROWS, C), BF16), pltpu.VMEM((2, ROWS, C), BF16), pltpu.VMEM((8, C), F32),
-            pltpu.VMEM((2, 4 * ROWS, HALF), BF16), pltpu.VMEM((2, 4 * ROWS, HALF), BF16),
+            pltpu.VMEM((2, 4 * ROWS, HALF), BF16), pltpu.VMEM((2, HALF, 4 * ROWS), BF16),
+            pltpu.VMEM((2, 4 * ROWS, HALF), BF16),
             pltpu.VMEM((2, HALF, HALF), BF16), pltpu.VMEM((2, HALF // 2, HALF), BF16),
-            pltpu.VMEM((2, 3, BLOCK, HALF), BF16), pltpu.VMEM((2, HALF, C), BF16), pltpu.VMEM((256, C), F32),
-            pltpu.VMEM((2, OUT_ROWS, C), F32), pltpu.VMEM((2, OUT_ROWS, C), F32), pltpu.VMEM((2, OUT_ROWS, C), F32),
-            dma((2, 4)), dma((2, PIECES)), dma((2, PIECES)), dma((2, 3)), dma((2, 3)),
+            pltpu.VMEM((2, 3, BLOCK, HALF), BF16), pltpu.VMEM((2, HALF // 2, C), BF16), pltpu.VMEM((256, C), F32),
+            pltpu.VMEM((2, OUT_ROWS, C), F32), pltpu.VMEM((2, 3, OUT_ROWS, C), BF16),
+            pltpu.VMEM((2, 3, OUT_ROWS, C), BF16),
+            dma((2, 4)), dma((2, PIECES, SPLIT)), dma((2, PIECES, SPLIT)), dma((2, 3)), dma((2, 3)),
             dma((2, 3, PIECES)), dma((2, 3, PIECES)), dma((2, 4)), dma((2, 4)), dma((2, 3)), dma((2, 3)),
-            dma((2, 3)), dma((2, 3)), dma((2, 4)), dma((2, 4)), dma((2, 8)), dma((2, 8)), dma((2,)), dma((2,)),
+            dma((2, 3)), dma((2, 3)), dma((2, 4)), dma((2, 4)), dma((2, 3)), dma((2, 3)),
         ],
         compiler_params=pltpu.CompilerParams(
-            collective_id=0, has_side_effects=True, vmem_limit_bytes=60 * 1024 * 1024
+            collective_id=0, has_side_effects=True, vmem_limit_bytes=40 * 1024 * 1024
         ),
     )(
-        emb, enc_weight.reshape(C, C), dec_weight.reshape(C, C), modulation.reshape(2, 256, C),
-        enc_inputs.reshape(ROWS, C), dec_inputs.reshape(ROWS, C), cotangent.reshape(ROWS, C),
+        emb, *[pltpu.with_memory_space_constraint(a, pltpu.HBM) for a in (enc_weight.reshape(C, C), dec_weight.reshape(C, C), modulation.reshape(2, 256, C),
+        enc_inputs.reshape(ROWS, C), dec_inputs.reshape(ROWS, C), cotangent.reshape(ROWS, C))],
     )
     return out.reshape(1, 2, 1, ROWS // 2, C), grams[None]
 

time: 166 us -> 140 us (0.84)
  Pallas kernels: 160 us -> 137 us
  local copies, waits for them, and re-layouts: 3.7 us -> 1.62 us
    pallas_call x1, Pallas kernels: 160 us -> 137 us  [body(): pl.pallas_call(kernel, name='unet_backward', out_shape=(jax.ShapeDtypeStr...]
    unnamed x2, local copies, waits for them, and re-layouts: 3.62 us -> 1.53 us
where the time goes in v2:
time: 140 us
  Pallas kernels  137 us (98%)
  local copies, waits for them, and re-layouts  1.62 us (1%)
    pallas_call x1, Pallas kernels, body(): pl.pallas_call(kernel, name='unet_backward', out_shape=(jax.ShapeDtypeStr...  137 us

profile of v2, /device:TPU:1, one launch (start us, length us, event | category | flops | bytes accessed | tf_op | source)
XLA Modules:
  0.0 139.9 jit_solution(2211751922732811100)
XLA Ops:
  0.6 0.7 convert_reduce_fusion
  1.3 0.1 convert_element_type.18
  1.4 0.1 multiply_sine_fusion
  1.5 136.8 %unet_backward.1 = (bf16[192,1280]{1,0:T(8,128)(2,1)S(1)}, f32[2,40,1280]{2,1,0:T(8,128)S(1)}) custom-call(f32[8,256]{1,0:T(8,128)S(1)} %pad_maximum_fusion.emb_ref, bf16[1280,1280]{1,0:T(8,128)(2,1)} %bitcast.12, bf16[1280,1280]{1,0:T(8,128)(2,1)} %bitcast.13, bf16[2,256,1280]{2,1,0:T(8,128)(2,1)} %bitcast.14, bf16[192,1280]{1,0:T(8,128)(2,1)} %bitcast.15, ...), custom_call_target="tpu_custom_call" | custom-call | tf_op jit(solution)/shard_map/unet_backward/pallas_call | solution.py:402
  138.3 0.8 copy.12
  139.1 0.8 copy.13
  (2 shorter events, 0.0 us)

commit v3 on v2

--- a/solution.py
+++ b/solution.py
@@ -20,8 +20,8 @@
 LEVELS = 8
 BLOCK = 80
 OUT_ROWS = 40
-PHASES = 7
-EARLY = (6, 6, 5, 4, 2, 2, 1, 1)
+PHASES = 6
+EARLY = (3, 3, 3, 1, 1, 0, 0, 0)
 DENOM = 7864320.0
 ENC, DEC = 0, 1
 
@@ -29,7 +29,7 @@
 def kernel(
     emb_ref, enc_w, dec_w, mod_hbm, enc_u, dec_u, cot_hbm, out_ref, gram_ref,
     w, wt, mod, u, sg, chain_in, back, delta, gains,
-    u4, u4t, d4, part, from_rep, from_z, g, gram_acc, own_gram, send_gram, recv_gram,
+    u4, d4, part, from_rep, from_z, g, gram_acc, own_gram, send_gram, recv_gram,
     load_sem, chain_s, chain_r, u_s, u_r, d_s, d_r, x_s, x_r, z_s, z_r,
     az_s, az_r, ac_s, ac_r, f_s, f_r,
 ):
@@ -199,28 +199,20 @@
         def _():
             for q in range(3):
                 u_copy(side, q).wait_recv()
-            u4t[side] = u4[side].T
-
-        @pl.when(p == 1)
-        def _():
-            for q in range(3):
 
                 def one(m, carry):
                     delta_copy(side, m, q).wait_recv()
                     return carry
 
                 lax.fori_loop(0, PIECES, one, 0)
-            for rr in (1 - r, r):
-                at = rows(rr * (HALF // 2), HALF // 2, 16)
-                part[side, at, :] = jnp.dot(
-                    u4t[side, at, :], d4[side], preferred_element_type=F32
-                ).astype(BF16)
-                if rr is not r:
-                    for j in range(3):
-                        x_copy(side, zg_of[j]).start()
-                    x_copy(side, zg).start()
-
-        @pl.when(p == 2)
+            part[side] = lax.dot_general(
+                u4[side], d4[side], (((0,), (0,)), ((), ())), preferred_element_type=F32
+            ).astype(BF16)
+            for j in range(3):
+                x_copy(side, zg_of[j]).start()
+            x_copy(side, zg).start()
+
+        @pl.when(p == 1)
         def _():
             for j in range(3):
                 x_copy(side, zg_of[j]).wait_recv()
@@ -231,7 +223,7 @@
                 ).astype(BF16)
                 z_copy(side, j).start()
 
-        @pl.when(p == 3)
+        @pl.when(p == 2)
         def _():
             x_copy(side, zg).wait_recv()
             total = part[side, piece_rows(r, zg), :].astype(F32) + from_rep[
@@ -245,13 +237,13 @@
                 az_copy(side, j).start()
             ac_copy(side, zg).start()
 
-        @pl.when(p == 4)
+        @pl.when(p == 3)
         def _():
             for j in range(3):
                 az_copy(side, 2 - j).wait_recv()
                 ac_copy(side, zg_of[j]).start()
 
-        @pl.when(p == 5)
+        @pl.when(p == 4)
         def _():
             for zz in range(4):
                 ac_copy(side, zz).wait_recv()
@@ -275,7 +267,7 @@
 
             lax.fori_loop(0, 2, there, 0)
 
-        @pl.when(p == 6)
+        @pl.when(p == 5)
         def _():
             gram = own_gram[side]
             for j in range(3):
@@ -287,10 +279,9 @@
     for level_index, count in enumerate(EARLY):
         early = jnp.where(s == level_index, count, early)
 
-    def step(t, carry):
-        i = jnp.maximum(t, 1) - 1
+    def step(i, carry):
         last = s == LEVELS - 1
-        is_chain = (t > 0) & (t <= 2 * PIECES)
+        is_chain = i < 2 * PIECES
         is_dec = is_chain & jnp.where(last, i % 2 == 0, i < PIECES)
         is_enc = is_chain & jnp.where(last, i % 2 == 1, i >= PIECES)
         m = jnp.where(last, lax.div(i, 2), lax.rem(i, PIECES))
@@ -323,21 +314,14 @@
             share_delta(ENC, m)
             out_ref[at, :] = back[ENC, at, :]
 
-        first = t == 0
-        middle = t == PIECES
-        late = t > 2 * PIECES
-        front = s < 4
-        lead = jnp.where(s == 0, 2, 1)
-        n = jnp.where(
-            first,
-            jnp.where(front, 0, 2),
-            jnp.where(middle, jnp.where(front, lead + early, early - 1), jnp.where(late, 2, 0)),
-        )
+        middle = i == PIECES - 1
+        late = i >= 2 * PIECES
+        lead = jnp.where(s == 0, 1, 0)
+        n = jnp.where(middle, lead + early, jnp.where(late, 2, 0))
 
         def event(j, carry):
-            p_middle = jnp.where(front, jnp.where(j < lead, j + 1 - lead, j - lead), j + 1)
-            p = jnp.where(first, 0, jnp.where(middle, p_middle, t - 2 * PIECES))
-            side = jnp.where(middle, jnp.where(front & (j < lead), ENC, DEC), 1 - j)
+            p = jnp.where(middle, j - lead, i - 2 * PIECES)
+            side = jnp.where(middle, jnp.where(p < 0, ENC, DEC), 1 - j)
             done = late & (side == DEC) & (p < early)
 
             @pl.when(jnp.logical_not(done))
@@ -409,8 +393,7 @@
             pltpu.VMEM((2, C, C), BF16), pltpu.VMEM((2, C, C), BF16), pltpu.VMEM((2, 256, C), BF16),
             pltpu.VMEM((2, ROWS, C), BF16), pltpu.VMEM((2, ROWS, C), F32), pltpu.VMEM((2, ROWS, C), BF16),
             pltpu.VMEM((2, ROWS, C), BF16), pltpu.VMEM((2, ROWS, C), BF16), pltpu.VMEM((8, C), F32),
-            pltpu.VMEM((2, 4 * ROWS, HALF), BF16), pltpu.VMEM((2, HALF, 4 * ROWS), BF16),
-            pltpu.VMEM((2, 4 * ROWS, HALF), BF16),
+            pltpu.VMEM((2, 4 * ROWS, HALF), BF16), pltpu.VMEM((2, 4 * ROWS, HALF), BF16),
             pltpu.VMEM((2, HALF, HALF), BF16), pltpu.VMEM((2, HALF // 2, HALF), BF16),
             pltpu.VMEM((2, 3, BLOCK, HALF), BF16), pltpu.VMEM((2, HALF // 2, C), BF16), pltpu.VMEM((256, C), F32),
             pltpu.VMEM((2, OUT_ROWS, C), F32), pltpu.VMEM((2, 3, OUT_ROWS, C), BF16),

time: 140 us -> 132 us (0.943)
  Pallas kernels: 137 us -> 129 us
    pallas_call x1, Pallas kernels: 137 us -> 129 us  [body(): pl.pallas_call(kernel, name='unet_backward', out_shape=(jax.ShapeDtypeStr...]
where the time goes in v3:
time: 132 us
  Pallas kernels  129 us (98%)
  local copies, waits for them, and re-layouts  1.62 us (1%)
    pallas_call x1, Pallas kernels, body(): pl.pallas_call(kernel, name='unet_backward', out_shape=(jax.ShapeDtypeStr...  129 us

profile of v3, /device:TPU:1, one launch (start us, length us, event | category | flops | bytes accessed | tf_op | source)
XLA Modules:
  0.0 131.8 jit_solution(4473216161225117558)
XLA Ops:
  0.6 0.7 convert_reduce_fusion
  1.3 0.1 convert_element_type.18
  1.4 0.1 multiply_sine_fusion
  1.5 128.7 %unet_backward.1 = (bf16[192,1280]{1,0:T(8,128)(2,1)S(1)}, f32[2,40,1280]{2,1,0:T(8,128)S(1)}) custom-call(f32[8,256]{1,0:T(8,128)S(1)} %pad_maximum_fusion.emb_ref, bf16[1280,1280]{1,0:T(8,128)(2,1)} %bitcast.12, bf16[1280,1280]{1,0:T(8,128)(2,1)} %bitcast.13, bf16[2,256,1280]{2,1,0:T(8,128)(2,1)} %bitcast.14, bf16[192,1280]{1,0:T(8,128)(2,1)} %bitcast.15, ...), custom_call_target="tpu_custom_call" | custom-call | tf_op jit(solution)/shard_map/unet_backward/pallas_call | solution.py:386
  130.3 0.8 copy.12
  131.0 0.8 copy.13
  (2 shorter events, 0.0 us)

commit v4 on v3

--- a/solution.py
+++ b/solution.py
@@ -21,6 +21,8 @@
 BLOCK = 80
 OUT_ROWS = 40
 PHASES = 6
+REP_FIRST = 512
+Z_FIRST = HALF - REP_FIRST
 EARLY = (3, 3, 3, 1, 1, 0, 0, 0)
 DENOM = 7864320.0
 ENC, DEC = 0, 1
@@ -29,8 +31,8 @@
 def kernel(
     emb_ref, enc_w, dec_w, mod_hbm, enc_u, dec_u, cot_hbm, out_ref, gram_ref,
     w, wt, mod, u, sg, chain_in, back, delta, gains,
-    u4, d4, part, from_rep, from_z, g, gram_acc, own_gram, send_gram, recv_gram,
-    load_sem, chain_s, chain_r, u_s, u_r, d_s, d_r, x_s, x_r, z_s, z_r,
+    u4, d4, part, from_rep, from_z, from_z_both, from_rep_late, g, gram_acc, own_gram, send_gram, recv_gram,
+    load_sem, chain_s, chain_r, u_s, u_r, d_s, d_r, x_s, x_r, z_s, z_r, zb_s, zb_r, xb_s, xb_r,
     az_s, az_r, ac_s, ac_r, f_s, f_r,
 ):
     s = lax.axis_index("section")
@@ -158,14 +160,33 @@
 
     def x_copy(side, zz):
         return remote(
-            part.at[side, piece_rows(1 - r, zz)], from_rep.at[side, rows(zz * BLOCK, BLOCK, 16)],
+            part.at[side, piece_rows(1 - r, zz), pl.ds(0, REP_FIRST)], from_rep.at[side, rows(zz * BLOCK, BLOCK, 16)],
             x_s.at[side, zz], x_r.at[side, zz], rep_other,
         )
 
     def z_copy(side, j):
         return remote(
-            part.at[side, piece_rows(r, zg_of[j])], from_z.at[side, 2 - j], z_s.at[side, j], z_r.at[side, 2 - j], z_group[j]
-        )
+            part.at[side, piece_rows(r, zg_of[j]), pl.ds(0, REP_FIRST)], from_z.at[side, 2 - j],
+            z_s.at[side, j], z_r.at[side, 2 - j], z_group[j],
+        )
+
+    def zb_copy(side, j, rr):
+        return remote(
+            part.at[side, piece_rows(rr, zg_of[j]), pl.ds(REP_FIRST, Z_FIRST)], from_z_both.at[side, 2 - j, rr],
+            zb_s.at[side, j, rr], zb_r.at[side, 2 - j, rr], z_group[j],
+        )
+
+    def xb_copy(side):
+        return remote(
+            part.at[side, piece_rows(1 - r, zg), pl.ds(REP_FIRST, Z_FIRST)], from_rep_late.at[side],
+            xb_s.at[side], xb_r.at[side], rep_other,
+        )
+
+    def z_first_sum(side, rr):
+        total = part[side, piece_rows(rr, zg), pl.ds(REP_FIRST, Z_FIRST)].astype(F32)
+        for j in range(3):
+            total = total + from_z_both[side, j, rr].astype(F32)
+        return total
 
     def g_piece(side, zz):
         return g.at[side, rows(zz * BLOCK, BLOCK, 16), col(c)]
@@ -210,6 +231,8 @@
             ).astype(BF16)
             for j in range(3):
                 x_copy(side, zg_of[j]).start()
+                zb_copy(side, j, 0).start()
+                zb_copy(side, j, 1).start()
             x_copy(side, zg).start()
 
         @pl.when(p == 1)
@@ -217,22 +240,31 @@
             for j in range(3):
                 x_copy(side, zg_of[j]).wait_recv()
                 at = piece_rows(r, zg_of[j])
-                part[side, at, :] = (
-                    part[side, at, :].astype(F32)
+                part[side, at, pl.ds(0, REP_FIRST)] = (
+                    part[side, at, pl.ds(0, REP_FIRST)].astype(F32)
                     + from_rep[side, rows(zg_of[j] * BLOCK, BLOCK, 16), :].astype(F32)
                 ).astype(BF16)
                 z_copy(side, j).start()
+            for j in range(3):
+                zb_copy(side, 2 - j, 0).wait_recv()
+                zb_copy(side, 2 - j, 1).wait_recv()
+            part[side, piece_rows(1 - r, zg), pl.ds(REP_FIRST, Z_FIRST)] = z_first_sum(side, 1 - r).astype(BF16)
+            xb_copy(side).start()
 
         @pl.when(p == 2)
         def _():
             x_copy(side, zg).wait_recv()
-            total = part[side, piece_rows(r, zg), :].astype(F32) + from_rep[
+            total = part[side, piece_rows(r, zg), pl.ds(0, REP_FIRST)].astype(F32) + from_rep[
                 side, rows(zg * BLOCK, BLOCK, 16), :
             ].astype(F32)
             for j in range(3):
                 z_copy(side, 2 - j).wait_recv()
                 total = total + from_z[side, j].astype(F32)
-            g[side, rows(zg * BLOCK, BLOCK, 16), col(c)] = total.astype(BF16)
+            xb_copy(side).wait_recv()
+            late_total = z_first_sum(side, r) + from_rep_late[side].astype(F32)
+            at = rows(zg * BLOCK, BLOCK, 16)
+            g[side, at, pl.ds(pl.multiple_of(c * HALF, 128), REP_FIRST)] = total.astype(BF16)
+            g[side, at, pl.ds(pl.multiple_of(c * HALF + REP_FIRST, 128), Z_FIRST)] = late_total.astype(BF16)
             for j in range(3):
                 az_copy(side, j).start()
             ac_copy(side, zg).start()
@@ -370,8 +402,11 @@
 
         for j in range(3):
             z_copy(side, j).wait_send()
+            zb_copy(side, j, 0).wait_send()
+            zb_copy(side, j, 1).wait_send()
             az_copy(side, j).wait_send()
             f_copy(side, j).wait_send()
+        xb_copy(side).wait_send()
         for zz in range(4):
             x_copy(side, zz).wait_send()
             ac_copy(side, zz).wait_send()
@@ -394,12 +429,14 @@
             pltpu.VMEM((2, ROWS, C), BF16), pltpu.VMEM((2, ROWS, C), F32), pltpu.VMEM((2, ROWS, C), BF16),
             pltpu.VMEM((2, ROWS, C), BF16), pltpu.VMEM((2, ROWS, C), BF16), pltpu.VMEM((8, C), F32),
             pltpu.VMEM((2, 4 * ROWS, HALF), BF16), pltpu.VMEM((2, 4 * ROWS, HALF), BF16),
-            pltpu.VMEM((2, HALF, HALF), BF16), pltpu.VMEM((2, HALF // 2, HALF), BF16),
-            pltpu.VMEM((2, 3, BLOCK, HALF), BF16), pltpu.VMEM((2, HALF // 2, C), BF16), pltpu.VMEM((256, C), F32),
+            pltpu.VMEM((2, HALF, HALF), BF16), pltpu.VMEM((2, HALF // 2, REP_FIRST), BF16),
+            pltpu.VMEM((2, 3, BLOCK, REP_FIRST), BF16),
+            pltpu.VMEM((2, 3, 2, BLOCK, Z_FIRST), BF16), pltpu.VMEM((2, BLOCK, Z_FIRST), BF16), pltpu.VMEM((2, HALF // 2, C), BF16), pltpu.VMEM((256, C), F32),
             pltpu.VMEM((2, OUT_ROWS, C), F32), pltpu.VMEM((2, 3, OUT_ROWS, C), BF16),
             pltpu.VMEM((2, 3, OUT_ROWS, C), BF16),
             dma((2, 4)), dma((2, PIECES, SPLIT)), dma((2, PIECES, SPLIT)), dma((2, 3)), dma((2, 3)),
             dma((2, 3, PIECES)), dma((2, 3, PIECES)), dma((2, 4)), dma((2, 4)), dma((2, 3)), dma((2, 3)),
+            dma((2, 3, 2)), dma((2, 3, 2)), dma((2,)), dma((2,)),
             dma((2, 3)), dma((2, 3)), dma((2, 4)), dma((2, 4)), dma((2, 3)), dma((2, 3)),
         ],
         compiler_params=pltpu.CompilerParams(

time: 132 us -> 130 us (0.985)
  Pallas kernels: 129 us -> 127 us
    pallas_call x1, Pallas kernels: 129 us -> 127 us  [body(): pl.pallas_call(kernel, name='unet_backward', out_shape=(jax.ShapeDtypeStr...]
where the time goes in v4:
time: 130 us
  Pallas kernels  127 us (98%)
  local copies, waits for them, and re-layouts  1.62 us (1%)
    pallas_call x1, Pallas kernels, body(): pl.pallas_call(kernel, name='unet_backward', out_shape=(jax.ShapeDtypeStr...  127 us

profile of v4, /device:TPU:1, one launch (start us, length us, event | category | flops | bytes accessed | tf_op | source)
XLA Modules:
  0.0 129.8 jit_solution(2236959749713243652)
XLA Ops:
  0.6 0.7 convert_reduce_fusion
  1.3 0.1 convert_element_type.18
  1.4 0.1 multiply_sine_fusion
  1.5 126.7 %unet_backward.1 = (bf16[192,1280]{1,0:T(8,128)(2,1)S(1)}, f32[2,40,1280]{2,1,0:T(8,128)S(1)}) custom-call(f32[8,256]{1,0:T(8,128)S(1)} %pad_maximum_fusion.emb_ref, bf16[1280,1280]{1,0:T(8,128)(2,1)} %bitcast.12, bf16[1280,1280]{1,0:T(8,128)(2,1)} %bitcast.13, bf16[2,256,1280]{2,1,0:T(8,128)(2,1)} %bitcast.14, bf16[192,1280]{1,0:T(8,128)(2,1)} %bitcast.15, ...), custom_call_target="tpu_custom_call" | custom-call | tf_op jit(solution)/shard_map/unet_backward/pallas_call | solution.py:421
  128.3 0.8 copy.12
  129.1 0.8 copy.13
  (2 shorter events, 0.0 us)

commit v5 on v4

--- a/solution.py
+++ b/solution.py
@@ -226,14 +226,15 @@
                     return carry
 
                 lax.fori_loop(0, PIECES, one, 0)
-            part[side] = lax.dot_general(
-                u4[side], d4[side], (((0,), (0,)), ((), ())), preferred_element_type=F32
-            ).astype(BF16)
-            for j in range(3):
-                x_copy(side, zg_of[j]).start()
-                zb_copy(side, j, 0).start()
-                zb_copy(side, j, 1).start()
-            x_copy(side, zg).start()
+            for cols, copies in (
+                (pl.ds(0, REP_FIRST), [x_copy(side, zz) for zz in zg_of + [zg]]),
+                (pl.ds(REP_FIRST, Z_FIRST), [zb_copy(side, j, rr) for j in range(3) for rr in range(2)]),
+            ):
+                part[side, :, cols] = lax.dot_general(
+                    u4[side], d4[side, :, cols], (((0,), (0,)), ((), ())), preferred_element_type=F32
+                ).astype(BF16)
+                for copy in copies:
+                    copy.start()
 
         @pl.when(p == 1)
         def _():
@@ -265,13 +266,13 @@
             at = rows(zg * BLOCK, BLOCK, 16)
             g[side, at, pl.ds(pl.multiple_of(c * HALF, 128), REP_FIRST)] = total.astype(BF16)
             g[side, at, pl.ds(pl.multiple_of(c * HALF + REP_FIRST, 128), Z_FIRST)] = late_total.astype(BF16)
-            for j in range(3):
+            for j in (1, 0, 2):
                 az_copy(side, j).start()
             ac_copy(side, zg).start()
 
         @pl.when(p == 3)
         def _():
-            for j in range(3):
+            for j in (0, 2, 1):
                 az_copy(side, 2 - j).wait_recv()
                 ac_copy(side, zg_of[j]).start()
 

time: 130 us -> 130 us (level)
  no operation moved by 1% of the time
where the time goes in v5:
time: 130 us
  Pallas kernels  127 us (98%)
  local copies, waits for them, and re-layouts  1.62 us (1%)
    pallas_call x1, Pallas kernels, body(): pl.pallas_call(kernel, name='unet_backward', out_shape=(jax.ShapeDtypeStr...  127 us

profile of v5, /device:TPU:1, one launch (start us, length us, event | category | flops | bytes accessed | tf_op | source)
XLA Modules:
  0.0 130.1 jit_solution(12013492094736332349)
XLA Ops:
  0.6 0.7 convert_reduce_fusion
  1.3 0.1 convert_element_type.18
  1.4 0.1 multiply_sine_fusion
  1.5 127.0 %unet_backward.1 = (bf16[192,1280]{1,0:T(8,128)(2,1)S(1)}, f32[2,40,1280]{2,1,0:T(8,128)S(1)}) custom-call(f32[8,256]{1,0:T(8,128)S(1)} %pad_maximum_fusion.emb_ref, bf16[1280,1280]{1,0:T(8,128)(2,1)} %bitcast.12, bf16[1280,1280]{1,0:T(8,128)(2,1)} %bitcast.13, bf16[2,256,1280]{2,1,0:T(8,128)(2,1)} %bitcast.14, bf16[192,1280]{1,0:T(8,128)(2,1)} %bitcast.15, ...), custom_call_target="tpu_custom_call" | custom-call | tf_op jit(solution)/shard_map/unet_backward/pallas_call | solution.py:422
  128.6 0.8 copy.12
  129.3 0.8 copy.13
  (2 shorter events, 0.0 us)
